TPU v7x, 32 devices: a whole 2x2x4 slice. The times are simulated.
32 devices in a mesh: replica: 1, ep: 32 (over z, y, x, core).
Axes of the slice: x: 2, y: 2, z: 4, core: 2. Of those that a mesh axis runs over, the one named last changes fastest.
Arguments:
- tokens: bfloat16 [2, 512, 3584], P(None, ('replica', 'ep')), may hold values from -6 to 6
- routes: int32 [2, 512, 8], P(None, ('replica', 'ep')), may hold values from 0 to 31, all different within a row; in each aligned block of 16 rows (0 to 15, 16 to 31, ..., all dimensions but the last counted through in order) at most 8 rows name the same one
- gates: float32 [2, 512, 8], P(None, ('replica', 'ep')), may hold values from 0.1 to 1
- weights: bfloat16 [32, 3584, 1024], P('ep'), may hold values from -0.09375 to 0.09375
Outputs:
- mixed: bfloat16 [2, 512, 1024], P(None, ('replica', 'ep'))
Inputs may be any that keep to these rules, and one draw needn't show every extreme that they name: `routes`: each row names 8 different experts. In each micro-batch the 16 rows of one device name no expert more than 8 times, and in some of these blocks one expert exactly 8 times.
All inputs are finite; a program needn't handle non-finite values.
Results may differ from a plain program's by a relative error of at most 0.0095.
Values may be sent and summed in bfloat16 or wider, within the bound.
A program may use at most 64 MiB of HBM per device.

v0:
```python
import jax
import jax.numpy as jnp
from jax import lax
from jax.sharding import PartitionSpec as P


def shards(tokens, routes, gates, weights):
    n_ep = lax.axis_size("ep")
    local = weights.shape[0]
    experts = local * n_ep
    tok_rows = tokens.shape[1]
    top = routes.shape[2]
    width = tokens.shape[2]
    groups = width // 128
    cap = max(2, 2 * tok_rows * top // experts)
    micro_count = tokens.shape[0]
    outputs = []
    for micro in range(micro_count):
        grouped = tokens[micro].astype(jnp.float32).reshape(tok_rows, groups, 128)
        amax = jnp.max(jnp.abs(grouped), axis=2)
        scale = ((amax + 1e-06) / 448.0).astype(jnp.bfloat16)
        quant = (grouped / scale.astype(jnp.float32)[:, :, None]).astype(jnp.bfloat16)
        quant = quant.reshape(tok_rows, width)
        ids = routes[micro].reshape(-1)
        onehot = (ids[:, None] == jnp.arange(experts, dtype=jnp.int32)[None, :]).astype(jnp.int32)
        rank = jnp.sum(jnp.cumsum(onehot, axis=0) * onehot, axis=1) - 1
        prepare_slot = ids * cap + rank
        owner = (
            jnp.zeros((experts * cap,), jnp.int32)
            .at[prepare_slot]
            .set(jnp.arange(ids.shape[0], dtype=jnp.int32) // top)
        )
        filled = jnp.zeros((experts * cap,), jnp.bool_).at[prepare_slot].set(True)
        send_rows = jnp.where(filled[:, None], quant[owner], jnp.zeros((), jnp.bfloat16))
        send_scales = jnp.where(filled[:, None], scale[owner], jnp.zeros((), jnp.bfloat16))
        send_rows = send_rows.reshape(n_ep, local, cap, width)
        send_scales = send_scales.reshape(n_ep, local, cap, groups)
        send_rows, send_scales, slot = (send_rows, send_scales, prepare_slot)
        got_rows = lax.all_to_all(send_rows, "ep", split_axis=0, concat_axis=0, tiled=True)
        got_scales = lax.all_to_all(send_scales, "ep", split_axis=0, concat_axis=0, tiled=True)
        shape = got_rows.shape
        restored = got_rows.astype(jnp.float32).reshape(shape[:3] + (groups, 128))
        restored = (restored * got_scales.astype(jnp.float32)[..., None]).astype(jnp.bfloat16)
        restored = restored.reshape(shape)
        hidden = jnp.einsum("sjcd,jdf->sjcf", restored, weights, preferred_element_type=jnp.float32)
        answers = lax.all_to_all(
            jax.nn.silu(hidden).astype(jnp.bfloat16), "ep", split_axis=0, concat_axis=0, tiled=True
        )
        flat = answers.reshape(experts * cap, answers.shape[3])
        picked = flat[slot].reshape(tok_rows, top, flat.shape[1]).astype(jnp.float32)
        outputs.append(jnp.sum(gates[micro][:, :, None] * picked, axis=1).astype(jnp.bfloat16))
    return jnp.stack(outputs)


def solution(mesh):
    placed = (
        P(None, ("replica", "ep"), None),
        P(None, ("replica", "ep"), None),
        P(None, ("replica", "ep"), None),
        P("ep", None, None),
    )
    return jax.shard_map(
        shards,
        mesh=mesh,
        in_specs=placed,
        out_specs=P(None, ("replica", "ep"), None),
        check_vma=False,
    )
```

profile of v0, /device:TPU:0, one launch (start us, length us, event | category | flops | bytes accessed | tf_op | source)
XLA Modules:
  0.0 167.8 jit_solution(16383219328861982819)
XLA Ops:
  0.0 0.7 fusion.58
  1.5 1.0 scatter_custom_fusion.1
  2.5 1.0 convert_abs_fusion.1
  3.7 1.0 scatter_custom_fusion
  4.8 0.9 gather_fusion.1
  5.7 0.7 bitcast_select_fusion.3
  6.4 7.3 %all-to-all-start.1 = ((bf16[32,1,8,28]{3,2,1,0:T(8,128)(2,1)}), bf16[32,1,8,28]{3,2,1,0:T(8,128)(2,1)S(1)}, u32[]{:S(2)}, u32[]{:S(2)}) async-start(bf16[32,1,8,28]{3,2,1,0:T(8,128)(2,1)} %bitcast_select_fusion.3), calls=%async_computation.1 | async-start | bytes 131072 | tf_op jit(solution)/shard_map/all_to_all | solution.py:40
  14.5 1.0 scatter_custom_fusion.3
  15.5 1.0 scatter_custom_fusion.2
  16.8 0.9 gather_fusion.4
  18.3 0.7 bitcast_select_fusion.2
  19.0 1.7 %gather_fusion = bf16[256,3584]{1,0:T(8,128)(2,1)S(1)} fusion(bf16[16,3584]{1,0:T(8,128)(2,1)S(1)} %get-tuple-element.5, s32[1024]{0:T(1024)S(1)} %pad_clamp_fusion.3), kind=kCustom, calls=%fused_computation | custom fusion | bytes 3671040 | tf_op jit(solution)/shard_map/gather | solution.py:34
  20.7 0.4 all-to-all-done.1
  21.1 5.4 %all-to-all-start.4 = ((bf16[32,1,8,28]{3,2,1,0:T(8,128)(2,1)}), bf16[32,1,8,28]{3,2,1,0:T(8,128)(2,1)S(1)}, u32[]{:S(2)}, u32[]{:S(2)}) async-start(bf16[32,1,8,28]{3,2,1,0:T(8,128)(2,1)} %bitcast_select_fusion.2), calls=%async_computation.4 | async-start | bytes 131072 | tf_op jit(solution)/shard_map/all_to_all | solution.py:40
  26.6 1.4 bitcast_select_fusion.1
  28.0 6.0 %all-to-all-done.4 = bf16[32,1,8,28]{3,2,1,0:T(8,128)(2,1)S(1)} async-done(((bf16[32,1,8,28]{3,2,1,0:T(8,128)(2,1)}), bf16[32,1,8,28]{3,2,1,0:T(8,128)(2,1)S(1)}, u32[]{:S(2)}, u32[]{:S(2)}) %all-to-all-start.4) | async-done | bytes 14368 | tf_op jit(solution)/shard_map/all_to_all | solution.py:40
  34.0 3.4 %all-to-all-start = ((bf16[32,1,8,3584]{3,2,1,0:T(8,128)(2,1)}), bf16[32,1,8,3584]{3,2,1,0:T(8,128)(2,1)}, u32[]{:S(2)}, u32[]{:S(2)}) async-start(bf16[32,1,8,3584]{3,2,1,0:T(8,128)(2,1)} %bitcast_select_fusion.1), calls=%async_computation | async-start | bytes 3670016 | tf_op jit(solution)/shard_map/all_to_all | solution.py:39
  37.4 1.7 %gather_fusion.3 = bf16[256,3584]{1,0:T(8,128)(2,1)S(1)} fusion(bf16[16,3584]{1,0:T(8,128)(2,1)S(1)} %get-tuple-element.6, s32[1024]{0:T(1024)S(1)} %pad_clamp_fusion.1), kind=kCustom, calls=%fused_computation.3 | custom fusion | bytes 3671040 | tf_op jit(solution)/shard_map/gather | solution.py:34
  39.2 1.4 bitcast_select_fusion
  40.6 40.1 %all-to-all-done = bf16[32,1,8,3584]{3,2,1,0:T(8,128)(2,1)} async-done(((bf16[32,1,8,3584]{3,2,1,0:T(8,128)(2,1)}), bf16[32,1,8,3584]{3,2,1,0:T(8,128)(2,1)}, u32[]{:S(2)}, u32[]{:S(2)}) %all-to-all-start) | async-done | bytes 1835040 | tf_op jit(solution)/shard_map/all_to_all | solution.py:39
  80.7 3.9 %all-to-all-start.3 = ((bf16[32,1,8,3584]{3,2,1,0:T(8,128)(2,1)}), bf16[32,1,8,3584]{3,2,1,0:T(8,128)(2,1)S(1)}, u32[]{:S(2)}, u32[]{:S(2)}) async-start(bf16[32,1,8,3584]{3,2,1,0:T(8,128)(2,1)} %bitcast_select_fusion), calls=%async_computation.3 | async-start | bytes 3670016 | tf_op jit(solution)/shard_map/all_to_all | solution.py:39
  84.6 0.3 copy.26
  84.9 6.7 %fusion.35 = bf16[32,1,8,1024]{3,2,1,0:T(8,128)(2,1)} fusion(bf16[1,3584,1024]{2,1,0:T(8,128)(2,1)} %param.7, bf16[32,1,8,3584]{3,2,1,0:T(8,128)(2,1)} %all-to-all-done, f32[32,8,28]{1,2,0:T(8,128)S(1)} %copy.26), kind=kOutput, calls=%fused_computation.29 | convolution fusion | flops 1883111424 | bytes 9728000 | tf_op jit(solution)/shard_map/sjcd,jdf->sjcf/dot_general | solution.py:45
  91.6 36.2 %all-to-all-done.3 = bf16[32,1,8,3584]{3,2,1,0:T(8,128)(2,1)S(1)} async-done(((bf16[32,1,8,3584]{3,2,1,0:T(8,128)(2,1)}), bf16[32,1,8,3584]{3,2,1,0:T(8,128)(2,1)S(1)}, u32[]{:S(2)}, u32[]{:S(2)}) %all-to-all-start.3) | async-done | bytes 1835040 | tf_op jit(solution)/shard_map/all_to_all | solution.py:39
  127.8 4.2 %all-to-all-start.2 = ((bf16[32,1,8,1024]{3,2,1,0:T(8,128)(2,1)}), bf16[32,1,8,1024]{3,2,1,0:T(8,128)(2,1)S(1)}, u32[]{:S(2)}, u32[]{:S(2)}) async-start(bf16[32,1,8,1024]{3,2,1,0:T(8,128)(2,1)} %fusion.35), calls=%async_computation.2 | async-start | bytes 1048576 | tf_op jit(solution)/shard_map/all_to_all | solution.py:46
  132.3 6.1 %fusion.26 = bf16[32,1,8,1024]{3,2,1,0:T(8,128)(2,1)} fusion(bf16[1,3584,1024]{2,1,0:T(8,128)(2,1)} %param.7, bf16[32,1,8,3584]{3,2,1,0:T(8,128)(2,1)S(1)} %all-to-all-done.3, f32[32,8,28]{1,2,0:T(8,128)S(1)} %copy.33), kind=kOutput, calls=%fused_computation.28 | convolution fusion | flops 1883111424 | bytes 9728000 | tf_op jit(solution)/shard_map/sjcd,jdf->sjcf/dot_general | solution.py:45
  138.4 9.0 %all-to-all-done.2 = bf16[32,1,8,1024]{3,2,1,0:T(8,128)(2,1)S(1)} async-done(((bf16[32,1,8,1024]{3,2,1,0:T(8,128)(2,1)}), bf16[32,1,8,1024]{3,2,1,0:T(8,128)(2,1)S(1)}, u32[]{:S(2)}, u32[]{:S(2)}) %all-to-all-start.2) | async-done | bytes 524320 | tf_op jit(solution)/shard_map/all_to_all | solution.py:46
  147.4 3.1 %all-to-all-start.5 = ((bf16[32,1,8,1024]{3,2,1,0:T(8,128)(2,1)}), bf16[32,1,8,1024]{3,2,1,0:T(8,128)(2,1)S(1)}, u32[]{:S(2)}, u32[]{:S(2)}) async-start(bf16[32,1,8,1024]{3,2,1,0:T(8,128)(2,1)} %fusion.26), calls=%async_computation.5 | async-start | bytes 1048576 | tf_op jit(solution)/shard_map/all_to_all | solution.py:46
  150.7 0.9 gather_fusion.2
  151.8 14.3 %all-to-all-done.5 = bf16[32,1,8,1024]{3,2,1,0:T(8,128)(2,1)S(1)} async-done(((bf16[32,1,8,1024]{3,2,1,0:T(8,128)(2,1)}), bf16[32,1,8,1024]{3,2,1,0:T(8,128)(2,1)S(1)}, u32[]{:S(2)}, u32[]{:S(2)}) %all-to-all-start.5) | async-done | bytes 524320 | tf_op jit(solution)/shard_map/all_to_all | solution.py:46
  166.0 0.9 gather_fusion.5
  167.1 0.6 pad_maximum_fusion
  (47 shorter events, 3.6 us)
Async XLA Ops:
  3.5 14.5 %copy-start = (bf16[2,16,3584]{2,1,0:T(8,128)(2,1)S(1)}, bf16[2,16,3584]{2,1,0:T(8,128)(2,1)}, u32[]{:S(2)}) copy-start(bf16[2,16,3584]{2,1,0:T(8,128)(2,1)} %param.4) | copy-start | bytes 688132
  6.4 14.7 %all-to-all-start.1 = ((bf16[32,1,8,28]{3,2,1,0:T(8,128)(2,1)}), bf16[32,1,8,28]{3,2,1,0:T(8,128)(2,1)S(1)}, u32[]{:S(2)}, u32[]{:S(2)}) async-start(bf16[32,1,8,28]{3,2,1,0:T(8,128)(2,1)} %bitcast_select_fusion.3), calls=%async_computation.1 | async-start | bytes 131072 | tf_op jit(solution)/shard_map/all_to_all | solution.py:40
  21.1 12.9 %all-to-all-start.4 = ((bf16[32,1,8,28]{3,2,1,0:T(8,128)(2,1)}), bf16[32,1,8,28]{3,2,1,0:T(8,128)(2,1)S(1)}, u32[]{:S(2)}, u32[]{:S(2)}) async-start(bf16[32,1,8,28]{3,2,1,0:T(8,128)(2,1)} %bitcast_select_fusion.2), calls=%async_computation.4 | async-start | bytes 131072 | tf_op jit(solution)/shard_map/all_to_all | solution.py:40
  34.0 46.7 %all-to-all-start = ((bf16[32,1,8,3584]{3,2,1,0:T(8,128)(2,1)}), bf16[32,1,8,3584]{3,2,1,0:T(8,128)(2,1)}, u32[]{:S(2)}, u32[]{:S(2)}) async-start(bf16[32,1,8,3584]{3,2,1,0:T(8,128)(2,1)} %bitcast_select_fusion.1), calls=%async_computation | async-start | bytes 3670016 | tf_op jit(solution)/shard_map/all_to_all | solution.py:39
  80.7 47.1 %all-to-all-start.3 = ((bf16[32,1,8,3584]{3,2,1,0:T(8,128)(2,1)}), bf16[32,1,8,3584]{3,2,1,0:T(8,128)(2,1)S(1)}, u32[]{:S(2)}, u32[]{:S(2)}) async-start(bf16[32,1,8,3584]{3,2,1,0:T(8,128)(2,1)} %bitcast_select_fusion), calls=%async_computation.3 | async-start | bytes 3670016 | tf_op jit(solution)/shard_map/all_to_all | solution.py:39
  127.8 19.6 %all-to-all-start.2 = ((bf16[32,1,8,1024]{3,2,1,0:T(8,128)(2,1)}), bf16[32,1,8,1024]{3,2,1,0:T(8,128)(2,1)S(1)}, u32[]{:S(2)}, u32[]{:S(2)}) async-start(bf16[32,1,8,1024]{3,2,1,0:T(8,128)(2,1)} %fusion.35), calls=%async_computation.2 | async-start | bytes 1048576 | tf_op jit(solution)/shard_map/all_to_all | solution.py:46
  132.3 18.1 %copy-start.1 = (f32[2,16,8]{1,2,0:T(8,128)S(1)}, f32[2,16,8]{1,2,0:T(8,128)}, u32[]{:S(2)}) copy-start(f32[2,16,8]{1,2,0:T(8,128)} %param.6) | copy-start | bytes 3076
  147.4 18.6 %all-to-all-start.5 = ((bf16[32,1,8,1024]{3,2,1,0:T(8,128)(2,1)}), bf16[32,1,8,1024]{3,2,1,0:T(8,128)(2,1)S(1)}, u32[]{:S(2)}, u32[]{:S(2)}) async-start(bf16[32,1,8,1024]{3,2,1,0:T(8,128)(2,1)} %fusion.26), calls=%async_computation.5 | async-start | bytes 1048576 | tf_op jit(solution)/shard_map/all_to_all | solution.py:46
where the time goes:
time: 168 us
  waiting for transfers between devices  106 us (63%)
  starting transfers between devices  27.4 us (16%)
  local copies, waits for them, and re-layouts  12.8 us (8%)
  matrix products  12.8 us (8%)
  other arithmetic  8.62 us (5%)
    all_to_all x2, waiting for transfers between devices, shards(): lax.all_to_all(send_rows, 'ep', split_axis=0, concat_axis=0, tiled=True)  76.3 us
    all_to_all x2, waiting for transfers between devices, shards(): lax.all_to_all(jax.nn.silu(hidden).astype(jnp.bfloat16), 'ep', split_axis...  23.2 us
    dot_general x2, matrix products, shards(): jnp.einsum('sjcd,jdf->sjcf', restored, weights, preferred_element_type=jn...  12.8 us
    all_to_all x2, starting transfers between devices, shards(): lax.all_to_all(send_scales, 'ep', split_axis=0, concat_axis=0, tiled=True)  12.7 us
    all_to_all x2, starting transfers between devices, shards(): lax.all_to_all(send_rows, 'ep', split_axis=0, concat_axis=0, tiled=True)  7.34 us
    all_to_all x2, starting transfers between devices, shards(): lax.all_to_all(jax.nn.silu(hidden).astype(jnp.bfloat16), 'ep', split_axis...  7.28 us
    all_to_all x2, waiting for transfers between devices, shards(): lax.all_to_all(send_scales, 'ep', split_axis=0, concat_axis=0, tiled=True)  6.37 us
    gather x2, local copies, waits for them, and re-layouts, shards(): quant[owner]  3.44 us
  transfers between devices with their start and end apart: 6, of which 6 were waited for; matrix products, arithmetic and copies ran while one was open for 16% of the time, Pallas kernels for 0%

commit v1 on v0

v1 whole, which is shorter than its diff:
```python
import jax
import jax.numpy as jnp
from jax import lax
from jax.sharding import PartitionSpec as P


def restore(tokens):
    rows, width = tokens.shape
    grouped = tokens.astype(jnp.float32).reshape(rows, width // 128, 128)
    amax = jnp.max(jnp.abs(grouped), axis=2)
    scale = ((amax + 1e-06) / 448.0).astype(jnp.bfloat16).astype(jnp.float32)[:, :, None]
    quant = (grouped / scale).astype(jnp.bfloat16)
    return (quant.astype(jnp.float32) * scale).astype(jnp.bfloat16).reshape(rows, width)


def shards(tokens, routes, gates, weights):
    n_ep = lax.axis_size("ep")
    local = weights.shape[0]
    experts = local * n_ep
    micro, per, width = tokens.shape
    rows = micro * per
    restored = restore(tokens.reshape(rows, width))
    ids = routes.reshape(rows, -1)
    values = gates.reshape(rows, -1)
    names = jnp.arange(experts, dtype=jnp.int32)
    dense = jnp.sum(
        jnp.where(ids[:, :, None] == names[None, None, :], values[:, :, None], 0.0), axis=1
    )
    share = lax.all_to_all(
        dense.reshape(rows, n_ep, local), "ep", split_axis=1, concat_axis=0, tiled=True
    ).reshape(n_ep * rows, local)
    everyone = lax.all_gather(restored, "ep", axis=0, tiled=True)
    total = 0.0
    for j in range(local):
        hidden = jnp.dot(everyone, weights[j], preferred_element_type=jnp.float32)
        act = jax.nn.silu(hidden).astype(jnp.bfloat16).astype(jnp.float32)
        gate = share[:, j : j + 1]
        total = total + jnp.where(gate > 0.0, act, 0.0) * gate
    mixed = lax.psum_scatter(total, "ep", scatter_dimension=0, tiled=True)
    return mixed.astype(jnp.bfloat16).reshape(micro, per, -1)


def solution(mesh):
    placed = (
        P(None, ("replica", "ep"), None),
        P(None, ("replica", "ep"), None),
        P(None, ("replica", "ep"), None),
        P("ep", None, None),
    )
    return jax.shard_map(
        shards,
        mesh=mesh,
        in_specs=placed,
        out_specs=P(None, ("replica", "ep"), None),
        check_vma=False,
    )
```

time: 168 us -> 249 us (1.48)
  waiting for transfers between devices: 106 us -> 200 us
  starting transfers between devices: 27.4 us -> 0.04 us
  blocking collectives: 0 us -> 14.2 us
  between operations: 0.32 us -> 13.4 us
  local copies, waits for them, and re-layouts: 12.8 us -> 1.96 us
  other arithmetic: 8.62 us -> 4.79 us
    reduce_scatter x0 -> x1, waiting for transfers between devices: none -> 140 us  [shards(): mixed = lax.psum_scatter(total, 'ep', scatter_dimension=0, tiled=True)]
    all_to_all x6 -> x0, waiting for transfers between devices: 106 us -> none  [the longest x2 76.3 us: shards(): lax.all_to_all(send_rows, 'ep', split_axis=0, concat_axis=0, tiled=True)]
    all_gather x0 -> x1, waiting for transfers between devices: none -> 60.3 us  [shards(): everyone = lax.all_gather(restored, 'ep', axis=0, tiled=True)]
    all_to_all x6 -> x0, starting transfers between devices: 27.4 us -> none  [the longest x2 12.7 us: shards(): lax.all_to_all(send_scales, 'ep', split_axis=0, concat_axis=0, tiled=True)]
    all_to_all x0 -> x1, blocking collectives: none -> 14.2 us  [shards(): lax.all_to_all(dense.reshape(rows, n_ep, local), 'ep', split_axis=1, conc...]
    gather x6 -> x0, local copies, waits for them, and re-layouts: 6.88 us -> none  [the longest x2 3.44 us: shards(): quant[owner]]
    select_n x9 -> x0, other arithmetic: 4.35 us -> none  [the longest x2 2.87 us: shards(): jnp.where(filled[:, None], quant[owner], jnp.zeros((), jnp.bfloat16))]
    scatter x4 -> x0, local copies, waits for them, and re-layouts: 3.97 us -> none  [the longest x2 2.01 us: shards(): filled = jnp.zeros((experts * cap,), jnp.bool_).at[prepare_slot].set(True)]
  transfers between devices with their start and end apart: 6 -> 2, of which waited for: 6 -> 2; matrix products, arithmetic and copies ran while one was open for 16% -> 1% of each run, Pallas kernels for 0% -> 0%
where the time goes in v1:
time: 249 us
  waiting for transfers between devices  200 us (80%)
  blocking collectives  14.2 us (6%)
  matrix products  14.2 us (6%)
  between operations  13.4 us (5%)
  other arithmetic  4.79 us (2%)
    reduce_scatter x1, waiting for transfers between devices, shards(): mixed = lax.psum_scatter(total, 'ep', scatter_dimension=0, tiled=True)  140 us
    all_gather x1, waiting for transfers between devices, shards(): everyone = lax.all_gather(restored, 'ep', axis=0, tiled=True)  60.3 us
    all_to_all x1, blocking collectives, shards(): lax.all_to_all(dense.reshape(rows, n_ep, local), 'ep', split_axis=1, conc...  14.2 us
    dot_general x1, matrix products, shards(): hidden = jnp.dot(everyone, weights[j], preferred_element_type=jnp.float32)  14.2 us
  transfers between devices with their start and end apart: 2, of which 2 were waited for; matrix products, arithmetic and copies ran while one was open for 1% of the time, Pallas kernels for 0%

profile of v1, /device:TPU:0, one launch (start us, length us, event | category | flops | bytes accessed | tf_op | source)
XLA Modules:
  0.0 248.9 jit_solution(18341081661623890083)
XLA Ops:
  6.5 0.0 all-gather.2.cloned.1.call-start
  6.5 1.0 convert_abs_fusion
  7.5 0.1 abs.7
  7.6 0.2 reduce_max.9
  7.8 0.2 div.23
  8.0 1.9 fusion.7
  9.9 0.0 all-gather.2.cloned.1.call-update
  10.0 0.0 reduce-scatter.2.cloned.1.call-start
  10.0 0.8 copy.18
  10.8 0.8 copy.19
  11.6 0.1 select_reduce_fusion
  11.7 0.1 copy.17
  11.8 14.2 %all_to_all.15 = f32[32,32,1]{0,2,1:T(1,128)S(1)} all-to-all(f32[32,32,1]{0,2,1:T(1,128)S(1)} %copy.17), channel_id=1, replica_groups=mesh['replica'=1,'ep'=32] {'ep'}, dimensions={1} | all-to-all | bytes 8192 | tf_op jit(solution)/shard_map/all_to_all | solution.py:29
  26.0 0.1 reshape.38
  26.1 60.3 %all-gather.2.cloned.1.call-done = bf16[1024,3584]{1,0:T(8,128)(2,1)} async-done(((bf16[32,3584]{1,0:T(8,128)(2,1)}), bf16[1024,3584]{1,0:T(8,128)(2,1)}) %all-gather.2.cloned.1.call-update) | async-done | bytes 7340048 | tf_op jit(solution)/shard_map/all_gather | solution.py:32
  86.4 14.2 %select_multiply_fusion = f32[1024,1024]{1,0:T(8,128)} fusion(bf16[1024,3584]{1,0:T(8,128)(2,1)} %all-gather.2.cloned.1.call-done, bf16[1,3584,1024]{2,1,0:T(8,128)(2,1)} %param.7, f32[1024]{0:T(1024)S(1)} %reshape.38, pred[1024]{0:T(1024)(128)(4,1)S(1)} %broadcast_compare_fusion), kind=kOutput, calls=%fused_computation.2 | convolution fusion | flops 7524581376 | bytes 18879488 | tf_op jit(solution)/shard_map/dot_general | solution.py:35
  100.6 0.0 reduce-scatter.2.cloned.1.call-update
  100.6 139.9 %reduce-scatter.2.cloned.1.call-done = f32[32,1024]{1,0:T(8,128)} async-done(((f32[1024,1024]{1,0:T(8,128)}), f32[32,1024]{1,0:T(8,128)}) %reduce-scatter.2.cloned.1.call-update) | async-done | bytes 131088 | tf_op jit(solution)/shard_map/reduce_scatter | solution.py:39
  240.5 1.5 convert_element_type.56
  (2 shorter events, 0.0 us)
Async XLA Ops:
  6.5 79.9 %all-gather.2.cloned.1.call-start = ((), (), s32[]{:S(2)}) async-start(), calls=%async_computation.2 | async-start | bytes 7569408 | tf_op jit(solution)/shard_map/all_gather | solution.py:32
  10.0 230.6 %reduce-scatter.2.cloned.1.call-start = ((), (), s32[]{:S(2)}) async-start(), calls=%async_computation.3 | async-start | bytes 4325376 | tf_op jit(solution)/shard_map/reduce_scatter | solution.py:39
Sparse Core Ops, SparseCore 0:
  10.2 76.1 all-gather.1
  100.7 139.7 reduce-scatter.1

commit v2 on v1

--- a/solution.py
+++ b/solution.py
@@ -1,7 +1,261 @@
+import functools
+
 import jax
 import jax.numpy as jnp
 from jax import lax
+from jax.experimental import pallas as pl
+from jax.experimental.pallas import tpu as pltpu
 from jax.sharding import PartitionSpec as P
+
+
+MESH = pl.DeviceIdType.MESH
+
+
+def kernel(per, width, ff, experts, tok, routes, gates, w_hbm, out,
+           got, w, mine, cs, cr, p1s, p1r, p2s, p2r, tot, zs, zr, fs, fr,
+           w_sem, send_sem, got_sem, c_sem, p1_sem, p2_sem, z_sem, f_sem):
+    me = lax.axis_index("ep")
+    c, x, y, z = me % 2, (me // 2) % 2, (me // 4) % 2, me // 8
+    ox, oy, oc = 1 - x, 1 - y, 1 - c
+    half = ff // 2
+    quarter = 8 * per
+
+    def device(zz, yy, xx, cc):
+        return ((zz * 2 + yy) * 2 + xx) * 2 + cc
+
+    def place(yy, xx, h, cc, zz):
+        return (((yy * 2 + xx) * 2 + h) * 2 + cc) * 4 + zz
+
+    others = [(z + k) % 4 for k in range(4)]
+    earlier = [(z + 4 - k) % 4 for k in range(4)]
+    x_dev, y_dev, c_dev = device(z, y, ox, c), device(z, oy, x, c), device(z, y, x, oc)
+    z_dev = [device(others[k], y, x, c) for k in range(4)]
+
+    w_copy = pltpu.make_async_copy(w_hbm.at[0], w, w_sem)
+    w_copy.start()
+    barrier = pltpu.get_barrier_semaphore()
+    for dev in (x_dev, y_dev, c_dev, z_dev[1], z_dev[2], z_dev[3]):
+        pl.semaphore_signal(barrier, inc=1, device_id={"ep": dev}, device_id_type=MESH)
+
+    lane = lax.broadcasted_iota(jnp.int32, (per, 128), 1)
+    for h in range(2):
+        rows = pl.ds(pl.multiple_of(place(y, x, h, c, z) * per, per), per)
+        for g in range(width // 128):
+            v = tok[h, :, g * 128 : (g + 1) * 128].astype(jnp.float32)
+            amax = jnp.max(jnp.abs(v), axis=1, keepdims=True)
+            scale = ((amax + 1e-06) / 448.0).astype(jnp.bfloat16).astype(jnp.float32)
+            quant = (v / scale).astype(jnp.bfloat16).astype(jnp.float32)
+            got[rows, g * 128 : (g + 1) * 128] = (quant * scale).astype(jnp.bfloat16)
+        names, values = routes[h], gates[h]
+        high = jnp.zeros((per, 128), jnp.float32)
+        low = jnp.zeros((per, 128), jnp.float32)
+        for k in range(names.shape[1]):
+            name, value = names[:, k : k + 1], values[:, k : k + 1]
+            high = high + jnp.where(lane == name, value, 0.0)
+            low = low + jnp.where(lane - experts == name, value, 0.0)
+        low = low - low.astype(jnp.bfloat16).astype(jnp.float32)
+        got[rows, width : width + 128] = jnp.where(lane < experts, high, low).astype(jnp.bfloat16)
+
+    pl.semaphore_wait(barrier, 6)
+
+    copies = []
+
+    def send(src, dst, sem, dev):
+        copy = pltpu.make_async_remote_copy(
+            src_ref=src, dst_ref=dst, send_sem=send_sem.at[len(copies)], recv_sem=sem,
+            device_id={"ep": dev}, device_id_type=MESH,
+        )
+        copy.start()
+        copies.append(copy)
+
+    def landed(dst, sem):
+        pltpu.make_async_remote_copy(
+            src_ref=dst, dst_ref=dst, send_sem=send_sem.at[0], recv_sem=sem,
+            device_id={"ep": c_dev}, device_id_type=MESH,
+        ).wait_recv()
+
+    def block(spot):
+        return got.at[pl.ds(pl.multiple_of(spot * per, per), per)]
+
+    def pass_on(spot, devs):
+        for dev in devs:
+            send(block(spot), block(spot), got_sem.at[spot], dev)
+
+    def arrive(spot):
+        landed(block(spot), got_sem.at[spot])
+
+    def sibling_line(yy, xx):
+        for h in range(2):
+            for k in range(4):
+                arrive(place(yy, xx, h, oc, earlier[k]))
+
+    def compute(u, yy, xx):
+        base = place(yy, xx, 0, 0, 0) * per
+        rows = pl.ds(pl.multiple_of(base, 2 * quarter), 2 * quarter)
+        wide = lax.broadcasted_iota(jnp.int32, (2 * quarter, 128), 1)
+        share = got[rows, width : width + 128].astype(jnp.float32)
+        picked = (wide == me) | (wide == me + experts)
+        gate = jnp.sum(jnp.where(picked, share, 0.0), axis=1, keepdims=True)
+
+        def tile(col):
+            cols = pl.ds(pl.multiple_of(col, 256), 256)
+            v = jnp.dot(got[rows, :width], w[:, cols], preferred_element_type=jnp.float32)
+            return gate * (v / (1.0 + jnp.exp(-v)))
+
+        for j in range(half // 256):
+            cs[u, :, j * 256 : (j + 1) * 256] = tile(oc * half + j * 256).astype(jnp.bfloat16)
+        send(cs.at[u], cr.at[u], c_sem.at[u], c_dev)
+        for j in range(half // 256):
+            mine[u, :, j * 256 : (j + 1) * 256] = tile(c * half + j * 256)
+
+    for h in range(2):
+        pass_on(place(y, x, h, c, z), [x_dev, y_dev, z_dev[1], z_dev[2], z_dev[3], c_dev])
+    for k in range(1, 4):
+        for h in range(2):
+            spot = place(y, x, h, c, earlier[k])
+            arrive(spot)
+            pass_on(spot, [x_dev, y_dev, c_dev])
+
+    def neighbours(k):
+        spot = place(y, ox, 0, c, earlier[k])
+        arrive(spot)
+        pass_on(spot, [y_dev, c_dev])
+        spot = place(oy, x, 1, c, earlier[k])
+        arrive(spot)
+        pass_on(spot, [x_dev, c_dev])
+        spot = place(y, ox, 1, c, earlier[k])
+        arrive(spot)
+        pass_on(spot, [c_dev])
+        spot = place(oy, x, 0, c, earlier[k])
+        arrive(spot)
+        pass_on(spot, [c_dev])
+
+    neighbours(0)
+    w_copy.wait()
+    sibling_line(y, x)
+    compute(0, y, x)
+    for k in range(1, 4):
+        neighbours(k)
+    sibling_line(y, ox)
+    compute(1, y, ox)
+    sibling_line(oy, x)
+    compute(2, oy, x)
+
+    lo, hi = pl.ds(0, quarter), pl.ds(quarter, quarter)
+
+    def joined(u, rows):
+        return mine[u, rows] + cr[u, rows].astype(jnp.float32)
+
+    def first(i, u, rows, dev):
+        p1s[i] = joined(u, rows).astype(jnp.bfloat16)
+        send(p1s.at[i], p1r.at[i], p1_sem.at[i], dev)
+
+    for k in range(4):
+        for h in range(2):
+            spot = place(oy, ox, h, c, earlier[k])
+            arrive(spot)
+            pass_on(spot, [c_dev])
+    for u in range(3):
+        landed(cr.at[u], c_sem.at[u])
+    first(0, 2, lo, y_dev)
+    first(1, 1, hi, x_dev)
+    sibling_line(oy, ox)
+    compute(3, oy, ox)
+    landed(cr.at[3], c_sem.at[3])
+    first(2, 3, lo, y_dev)
+    first(3, 3, hi, x_dev)
+
+    landed(p1r.at[2], p1_sem.at[2])
+    p2s[0] = (joined(1, lo) + p1r[2].astype(jnp.float32)).astype(jnp.bfloat16)
+    send(p2s.at[0], p2r.at[0], p2_sem.at[0], x_dev)
+    landed(p1r.at[3], p1_sem.at[3])
+    p2s[1] = (joined(2, hi) + p1r[3].astype(jnp.float32)).astype(jnp.bfloat16)
+    send(p2s.at[1], p2r.at[1], p2_sem.at[1], y_dev)
+    landed(p1r.at[0], p1_sem.at[0])
+    tot[lo] = joined(0, lo) + p1r[0].astype(jnp.float32)
+    landed(p1r.at[1], p1_sem.at[1])
+    tot[hi] = joined(0, hi) + p1r[1].astype(jnp.float32)
+    landed(p2r.at[0], p2_sem.at[0])
+    tot[lo] = tot[lo] + p2r[0].astype(jnp.float32)
+    landed(p2r.at[1], p2_sem.at[1])
+    tot[hi] = tot[hi] + p2r[1].astype(jnp.float32)
+
+    def part(h, cc, zz):
+        return tot[pl.ds(pl.multiple_of(((h * 2 + cc) * 4 + zz) * per, per), per)]
+
+    for k in range(1, 4):
+        for h in range(2):
+            for cc in range(2):
+                at = (h * 2 + cc) * per
+                zs[k, at : at + per] = part(h, cc, others[k]).astype(jnp.bfloat16)
+        send(zs.at[k], zr.at[k], z_sem.at[k], z_dev[k])
+    for k in range(1, 4):
+        landed(zr.at[k], z_sem.at[k])
+
+    def final(h, cc):
+        total = part(h, cc, z)
+        for k in range(1, 4):
+            rows = pl.ds(pl.multiple_of((h * 2 + cc) * per, per), per)
+            total = total + zr[k, rows].astype(jnp.float32)
+        return total.astype(jnp.bfloat16)
+
+    for h in range(2):
+        fs[h] = final(h, oc)
+    send(fs, fr, f_sem, c_dev)
+    for h in range(2):
+        out[h, :, pl.ds(pl.multiple_of(c * half, half), half)] = final(h, c)
+    landed(fr, f_sem)
+    for h in range(2):
+        out[h, :, pl.ds(pl.multiple_of(oc * half, half), half)] = fr[h]
+    for copy in copies:
+        copy.wait_send()
+
+
+def fused(tokens, routes, gates, weights):
+    n_ep = lax.axis_size("ep")
+    micro, per, width = tokens.shape
+    ff = weights.shape[2]
+    half, quarter = ff // 2, 8 * per
+    bf, f32 = jnp.bfloat16, jnp.float32
+    vmem = pl.BlockSpec(memory_space=pltpu.VMEM)
+    return pl.pallas_call(
+        functools.partial(kernel, per, width, ff, n_ep),
+        out_shape=jax.ShapeDtypeStruct((micro, per, ff), bf),
+        in_specs=[vmem, vmem, vmem, pl.BlockSpec(memory_space=pl.ANY)],
+        out_specs=vmem,
+        scratch_shapes=[
+            pltpu.VMEM((n_ep * 2 * per, width + 128), bf),
+            pltpu.VMEM((width, ff), bf),
+            pltpu.VMEM((4, 2 * quarter, half), f32),
+            pltpu.VMEM((4, 2 * quarter, half), bf),
+            pltpu.VMEM((4, 2 * quarter, half), bf),
+            pltpu.VMEM((4, quarter, half), bf),
+            pltpu.VMEM((4, quarter, half), bf),
+            pltpu.VMEM((2, quarter, half), bf),
+            pltpu.VMEM((2, quarter, half), bf),
+            pltpu.VMEM((2 * quarter, half), f32),
+            pltpu.VMEM((4, 4 * per, half), bf),
+            pltpu.VMEM((4, 4 * per, half), bf),
+            pltpu.VMEM((2, per, half), bf),
+            pltpu.VMEM((2, per, half), bf),
+            pltpu.SemaphoreType.DMA,
+            pltpu.SemaphoreType.DMA((96,)),
+            pltpu.SemaphoreType.DMA((64,)),
+            pltpu.SemaphoreType.DMA((4,)),
+            pltpu.SemaphoreType.DMA((4,)),
+            pltpu.SemaphoreType.DMA((2,)),
+            pltpu.SemaphoreType.DMA((4,)),
+            pltpu.SemaphoreType.DMA,
+        ],
+        compiler_params=pltpu.CompilerParams(
+            collective_id=0, has_side_effects=True, vmem_limit_bytes=48 * 1024 * 1024
+        ),
+        cost_estimate=pl.CostEstimate(
+            flops=2 * n_ep * 2 * per * width * ff,
+            bytes_accessed=2 * width * ff,
+            transcendentals=n_ep * 2 * per * ff,
+        ),
+    )(tokens, routes, gates, weights)
 
 
 def restore(tokens):
@@ -47,8 +301,9 @@
         P(None, ("replica", "ep"), None),
         P("ep", None, None),
     )
+    small = mesh.shape["ep"] == 32 and mesh.shape["replica"] == 1
     return jax.shard_map(
-        shards,
+        fused if small else shards,
         mesh=mesh,
         in_specs=placed,
         out_specs=P(None, ("replica", "ep"), None),

time: 249 us -> 72 us (0.29)
  waiting for transfers between devices: 200 us -> 0 us
  Pallas kernels: 0 us -> 68.6 us
  matrix products: 14.2 us -> 0 us
  blocking collectives: 14.2 us -> 0 us
  between operations: 13.4 us -> 0.01 us
  other arithmetic: 4.79 us -> 0 us
    reduce_scatter x1 -> x0, waiting for transfers between devices: 140 us -> none  [shards(): mixed = lax.psum_scatter(total, 'ep', scatter_dimension=0, tiled=True)]
    pallas_call x0 -> x1, Pallas kernels: none -> 68.6 us  [fused(): pl.pallas_call(functools.partial(kernel, per, width, ff, n_ep), out_shape...]
    all_gather x1 -> x0, waiting for transfers between devices: 60.3 us -> none  [shards(): everyone = lax.all_gather(restored, 'ep', axis=0, tiled=True)]
    all_to_all x1 -> x0, blocking collectives: 14.2 us -> none  [shards(): lax.all_to_all(dense.reshape(rows, n_ep, local), 'ep', split_axis=1, conc...]
    dot_general x1 -> x0, matrix products: 14.2 us -> none  [shards(): hidden = jnp.dot(everyone, weights[j], preferred_element_type=jnp.float32)]
    convert_element_type x3 -> x0, other arithmetic: 3.45 us -> none  [the longest x1 1.91 us: restore(): (quant.astype(jnp.float32) * scale).astype(jnp.bfloat16)]
    unnamed x0 -> x5, local copies, waits for them, and re-layouts: none -> 3.11 us
  transfers between devices with their start and end apart: 2 -> 0, of which waited for: 2 -> 0; matrix products, arithmetic and copies ran while one was open for 1% -> 0% of each run, Pallas kernels for 0% -> 0%
where the time goes in v2:
time: 72 us; the launch traced here: 71.7 us
  Pallas kernels  68.6 us (95%)
  local copies, waits for them, and re-layouts  3.11 us (4%)
    pallas_call x1, Pallas kernels, fused(): pl.pallas_call(functools.partial(kernel, per, width, ff, n_ep), out_shape...  68.6 us
    unnamed x5, local copies, waits for them, and re-layouts  3.11 us

profile of v2, /device:TPU:0, one launch (start us, length us, event | category | flops | bytes accessed | tf_op | source)
XLA Modules:
  0.0 71.7 jit_solution(17135801506586284660)
XLA Ops:
  0.0 0.8 %copy.5.routes = s32[2,16,8]{2,1,0:T(8,128)S(1)} copy(s32[2,16,8]{1,2,0:T(8,128)} %param.5) | data formatting | bytes 2048 | tf_op args[1]
  0.8 0.8 %copy.6.gates = f32[2,16,8]{2,1,0:T(8,128)S(1)} copy(f32[2,16,8]{1,2,0:T(8,128)} %param.6) | data formatting | bytes 2048 | tf_op args[2]
  1.5 0.0 copy-start
  1.5 0.9 %copy-done = bf16[2,16,3584]{2,1,0:T(8,128)(2,1)S(1)} copy-done((bf16[2,16,3584]{2,1,0:T(8,128)(2,1)S(1)}, bf16[2,16,3584]{2,1,0:T(8,128)(2,1)}, u32[]{:S(2)}) %copy-start) | copy-done | bytes 229400
  2.5 68.6 %shard_map.46 = bf16[2,16,1024]{2,1,0:T(8,128)(2,1)S(1)} custom-call(bf16[2,16,3584]{2,1,0:T(8,128)(2,1)S(1)} %copy-done, s32[2,16,8]{2,1,0:T(8,128)S(1)} %copy.5.routes, f32[2,16,8]{2,1,0:T(8,128)S(1)} %copy.6.gates, bf16[1,3584,1024]{2,1,0:T(8,128)(2,1)} %w_hbm.1), custom_call_target="tpu_custom_call" | custom-call | flops 7516192768 | bytes 7340032 | tf_op jit(solution)/shard_map/pallas_call | solution.py:221
  71.1 0.6 copy.8
Async XLA Ops:
  1.5 0.9 %copy-start = (bf16[2,16,3584]{2,1,0:T(8,128)(2,1)S(1)}, bf16[2,16,3584]{2,1,0:T(8,128)(2,1)}, u32[]{:S(2)}) copy-start(bf16[2,16,3584]{2,1,0:T(8,128)(2,1)} %tok.1) | copy-start | bytes 688132

commit v3 on v2

--- a/solution.py
+++ b/solution.py
@@ -19,6 +19,7 @@
     ox, oy, oc = 1 - x, 1 - y, 1 - c
     half = ff // 2
     quarter = 8 * per
+    parts = half // 256
 
     def device(zz, yy, xx, cc):
         return ((zz * 2 + yy) * 2 + xx) * 2 + cc
@@ -27,7 +28,9 @@
         return (((yy * 2 + xx) * 2 + h) * 2 + cc) * 4 + zz
 
     others = [(z + k) % 4 for k in range(4)]
-    earlier = [(z + 4 - k) % 4 for k in range(4)]
+    far = z // 2
+    line = [z, z + 1 - 2 * (z % 2), 2 - far, 3 - 3 * far]
+    inner = (z == 1) | (z == 2)
     x_dev, y_dev, c_dev = device(z, y, ox, c), device(z, oy, x, c), device(z, y, x, oc)
     z_dev = [device(others[k], y, x, c) for k in range(4)]
 
@@ -58,15 +61,26 @@
 
     pl.semaphore_wait(barrier, 6)
 
-    copies = []
+    copies, inner_copies = [], []
+
+    def prepare(src, dst, sem, dev):
+        return pltpu.make_async_remote_copy(
+            src_ref=src, dst_ref=dst, send_sem=send_sem.at[len(copies) + len(inner_copies)],
+            recv_sem=sem, device_id={"ep": dev}, device_id_type=MESH,
+        )
 
     def send(src, dst, sem, dev):
-        copy = pltpu.make_async_remote_copy(
-            src_ref=src, dst_ref=dst, send_sem=send_sem.at[len(copies)], recv_sem=sem,
-            device_id={"ep": dev}, device_id_type=MESH,
-        )
+        copy = prepare(src, dst, sem, dev)
         copy.start()
         copies.append(copy)
+
+    def inner_on(spot, dev):
+        copy = prepare(block(spot), block(spot), got_sem.at[spot], dev)
+        inner_copies.append(copy)
+
+        @pl.when(inner)
+        def _():
+            copy.start()
 
     def landed(dst, sem):
         pltpu.make_async_remote_copy(
@@ -87,7 +101,7 @@
     def sibling_line(yy, xx):
         for h in range(2):
             for k in range(4):
-                arrive(place(yy, xx, h, oc, earlier[k]))
+                arrive(place(yy, xx, h, oc, line[k]))
 
     def compute(u, yy, xx):
         base = place(yy, xx, 0, 0, 0) * per
@@ -102,113 +116,143 @@
             v = jnp.dot(got[rows, :width], w[:, cols], preferred_element_type=jnp.float32)
             return gate * (v / (1.0 + jnp.exp(-v)))
 
-        for j in range(half // 256):
-            cs[u, :, j * 256 : (j + 1) * 256] = tile(oc * half + j * 256).astype(jnp.bfloat16)
-        send(cs.at[u], cr.at[u], c_sem.at[u], c_dev)
-        for j in range(half // 256):
-            mine[u, :, j * 256 : (j + 1) * 256] = tile(c * half + j * 256)
-
-    for h in range(2):
-        pass_on(place(y, x, h, c, z), [x_dev, y_dev, z_dev[1], z_dev[2], z_dev[3], c_dev])
-    for k in range(1, 4):
-        for h in range(2):
-            spot = place(y, x, h, c, earlier[k])
+        for j in range(parts):
+            cs[u, j] = tile(oc * half + j * 256).astype(jnp.bfloat16)
+            if u == 3:
+                send(cs.at[u, j], cr.at[u, j], c_sem.at[u + j], c_dev)
+                mine[u, j] = tile(c * half + j * 256)
+                if j > 0:
+                    start(j - 1)
+        if u < 3:
+            send(cs.at[u], cr.at[u], c_sem.at[u], c_dev)
+            for j in range(parts):
+                mine[u, j] = tile(c * half + j * 256)
+
+    def neighbours(k):
+        if k != 1:
+            spot = place(y, ox, 0, c, line[k])
             arrive(spot)
-            pass_on(spot, [x_dev, y_dev, c_dev])
-
-    def neighbours(k):
-        spot = place(y, ox, 0, c, earlier[k])
-        arrive(spot)
-        pass_on(spot, [y_dev, c_dev])
-        spot = place(oy, x, 1, c, earlier[k])
-        arrive(spot)
-        pass_on(spot, [x_dev, c_dev])
-        spot = place(y, ox, 1, c, earlier[k])
+            pass_on(spot, [y_dev, c_dev])
+            spot = place(oy, x, 1, c, line[k])
+            arrive(spot)
+            pass_on(spot, [x_dev, c_dev])
+        spot = place(y, ox, 1, c, line[k])
         arrive(spot)
         pass_on(spot, [c_dev])
-        spot = place(oy, x, 0, c, earlier[k])
+        spot = place(oy, x, 0, c, line[k])
         arrive(spot)
         pass_on(spot, [c_dev])
 
-    neighbours(0)
+    def diagonal(k):
+        for h in range(2):
+            spot = place(oy, ox, h, c, line[k])
+            arrive(spot)
+            pass_on(spot, [near, c_dev] if k == 0 else [c_dev])
+
+    near, across = device(line[1], y, x, c), device(3 - z, y, x, c)
+    for h in range(2):
+        spot = place(y, x, h, c, z)
+        pass_on(spot, [near])
+        inner_on(spot, across)
+        pass_on(spot, [x_dev, y_dev, c_dev])
+    for k in range(1, 4):
+        for h in range(2):
+            spot = place(y, x, h, c, line[k])
+            arrive(spot)
+            inner_on(spot, across if k == 1 else near)
+            pass_on(spot, [x_dev, y_dev, c_dev] if k > 1 else [(y_dev, x_dev)[h], c_dev])
+        neighbours(k - 1)
+    pass_on(place(y, ox, 0, c, z), [near])
+    pass_on(place(oy, x, 1, c, z), [near])
+    diagonal(0)
     w_copy.wait()
     sibling_line(y, x)
     compute(0, y, x)
-    for k in range(1, 4):
-        neighbours(k)
+    neighbours(3)
+    for spot in (place(y, ox, 0, c, line[1]), place(oy, x, 1, c, line[1])):
+        arrive(spot)
+        pass_on(spot, [c_dev])
     sibling_line(y, ox)
     compute(1, y, ox)
+    diagonal(2)
     sibling_line(oy, x)
     compute(2, oy, x)
+    diagonal(1)
+    diagonal(3)
 
     lo, hi = pl.ds(0, quarter), pl.ds(quarter, quarter)
 
-    def joined(u, rows):
-        return mine[u, rows] + cr[u, rows].astype(jnp.float32)
-
-    def first(i, u, rows, dev):
-        p1s[i] = joined(u, rows).astype(jnp.bfloat16)
-        send(p1s.at[i], p1r.at[i], p1_sem.at[i], dev)
-
-    for k in range(4):
-        for h in range(2):
-            spot = place(oy, ox, h, c, earlier[k])
-            arrive(spot)
-            pass_on(spot, [c_dev])
+    def joined(u, j, rows):
+        return mine[u, j, rows] + cr[u, j, rows].astype(jnp.float32)
+
+    def first(i, j, u, rows, dev):
+        p1s[i, j] = joined(u, j, rows).astype(jnp.bfloat16)
+        send(p1s.at[i, j], p1r.at[i, j], p1_sem.at[i * parts + j], dev)
+
+    def start(j):
+        landed(cr.at[3, j], c_sem.at[3 + j])
+        first(2, j, 3, lo, y_dev)
+        first(3, j, 3, hi, x_dev)
+
     for u in range(3):
         landed(cr.at[u], c_sem.at[u])
-    first(0, 2, lo, y_dev)
-    first(1, 1, hi, x_dev)
+    for j in range(parts):
+        first(0, j, 2, lo, y_dev)
+        first(1, j, 1, hi, x_dev)
     sibling_line(oy, ox)
     compute(3, oy, ox)
-    landed(cr.at[3], c_sem.at[3])
-    first(2, 3, lo, y_dev)
-    first(3, 3, hi, x_dev)
-
-    landed(p1r.at[2], p1_sem.at[2])
-    p2s[0] = (joined(1, lo) + p1r[2].astype(jnp.float32)).astype(jnp.bfloat16)
-    send(p2s.at[0], p2r.at[0], p2_sem.at[0], x_dev)
-    landed(p1r.at[3], p1_sem.at[3])
-    p2s[1] = (joined(2, hi) + p1r[3].astype(jnp.float32)).astype(jnp.bfloat16)
-    send(p2s.at[1], p2r.at[1], p2_sem.at[1], y_dev)
-    landed(p1r.at[0], p1_sem.at[0])
-    tot[lo] = joined(0, lo) + p1r[0].astype(jnp.float32)
-    landed(p1r.at[1], p1_sem.at[1])
-    tot[hi] = joined(0, hi) + p1r[1].astype(jnp.float32)
-    landed(p2r.at[0], p2_sem.at[0])
-    tot[lo] = tot[lo] + p2r[0].astype(jnp.float32)
-    landed(p2r.at[1], p2_sem.at[1])
-    tot[hi] = tot[hi] + p2r[1].astype(jnp.float32)
-
-    def part(h, cc, zz):
-        return tot[pl.ds(pl.multiple_of(((h * 2 + cc) * 4 + zz) * per, per), per)]
-
-    for k in range(1, 4):
-        for h in range(2):
-            for cc in range(2):
-                at = (h * 2 + cc) * per
-                zs[k, at : at + per] = part(h, cc, others[k]).astype(jnp.bfloat16)
-        send(zs.at[k], zr.at[k], z_sem.at[k], z_dev[k])
-    for k in range(1, 4):
-        landed(zr.at[k], z_sem.at[k])
-
-    def final(h, cc):
-        total = part(h, cc, z)
+    start(parts - 1)
+
+    for j in range(parts):
+        for i, u, rows, dev in ((0, 1, lo, x_dev), (1, 2, hi, y_dev)):
+            landed(p1r.at[2 + i, j], p1_sem.at[(2 + i) * parts + j])
+            p2s[i, j] = (joined(u, j, rows) + p1r[2 + i, j].astype(jnp.float32)).astype(jnp.bfloat16)
+            send(p2s.at[i, j], p2r.at[i, j], p2_sem.at[i * parts + j], dev)
+    for j in range(parts):
+        for i, rows in ((0, lo), (1, hi)):
+            landed(p1r.at[i, j], p1_sem.at[i * parts + j])
+            tot[j, rows] = joined(0, j, rows) + p1r[i, j].astype(jnp.float32)
+
+    def part(j, h, cc, zz):
+        return tot[j, pl.ds(pl.multiple_of(((h * 2 + cc) * 4 + zz) * per, per), per)]
+
+    for j in range(parts):
+        for i, rows in ((0, lo), (1, hi)):
+            landed(p2r.at[i, j], p2_sem.at[i * parts + j])
+            tot[j, rows] = tot[j, rows] + p2r[i, j].astype(jnp.float32)
         for k in range(1, 4):
-            rows = pl.ds(pl.multiple_of((h * 2 + cc) * per, per), per)
-            total = total + zr[k, rows].astype(jnp.float32)
+            for h in range(2):
+                for cc in range(2):
+                    at = (h * 2 + cc) * per
+                    zs[k, j, at : at + per] = part(j, h, cc, others[k]).astype(jnp.bfloat16)
+            send(zs.at[k, j], zr.at[k, j], z_sem.at[k * parts + j], z_dev[k])
+
+    def final(j, h, cc):
+        total = part(j, h, cc, z)
+        rows = pl.ds(pl.multiple_of((h * 2 + cc) * per, per), per)
+        for k in range(1, 4):
+            total = total + zr[k, j, rows].astype(jnp.float32)
         return total.astype(jnp.bfloat16)
 
-    for h in range(2):
-        fs[h] = final(h, oc)
-    send(fs, fr, f_sem, c_dev)
-    for h in range(2):
-        out[h, :, pl.ds(pl.multiple_of(c * half, half), half)] = final(h, c)
-    landed(fr, f_sem)
-    for h in range(2):
-        out[h, :, pl.ds(pl.multiple_of(oc * half, half), half)] = fr[h]
+    for j in range(parts):
+        for k in range(1, 4):
+            landed(zr.at[k, j], z_sem.at[k * parts + j])
+        for h in range(2):
+            fs[j, h] = final(j, h, oc)
+        send(fs.at[j], fr.at[j], f_sem.at[j], c_dev)
+        for h in range(2):
+            out[h, :, pl.ds(pl.multiple_of(c * half + j * 256, 256), 256)] = final(j, h, c)
+    for j in range(parts):
+        landed(fr.at[j], f_sem.at[j])
+        for h in range(2):
+            out[h, :, pl.ds(pl.multiple_of(oc * half + j * 256, 256), 256)] = fr[j, h]
     for copy in copies:
         copy.wait_send()
+
+    @pl.when(inner)
+    def _():
+        for copy in inner_copies:
+            copy.wait_send()
 
 
 def fused(tokens, routes, gates, weights):
@@ -216,6 +260,7 @@
     micro, per, width = tokens.shape
     ff = weights.shape[2]
     half, quarter = ff // 2, 8 * per
+    parts = half // 256
     bf, f32 = jnp.bfloat16, jnp.float32
     vmem = pl.BlockSpec(memory_space=pltpu.VMEM)
     return pl.pallas_call(
@@ -226,26 +271,26 @@
         scratch_shapes=[
             pltpu.VMEM((n_ep * 2 * per, width + 128), bf),
             pltpu.VMEM((width, ff), bf),
-            pltpu.VMEM((4, 2 * quarter, half), f32),
-            pltpu.VMEM((4, 2 * quarter, half), bf),
-            pltpu.VMEM((4, 2 * quarter, half), bf),
-            pltpu.VMEM((4, quarter, half), bf),
-            pltpu.VMEM((4, quarter, half), bf),
-            pltpu.VMEM((2, quarter, half), bf),
-            pltpu.VMEM((2, quarter, half), bf),
-            pltpu.VMEM((2 * quarter, half), f32),
-            pltpu.VMEM((4, 4 * per, half), bf),
-            pltpu.VMEM((4, 4 * per, half), bf),
-            pltpu.VMEM((2, per, half), bf),
-            pltpu.VMEM((2, per, half), bf),
+            pltpu.VMEM((4, parts, 2 * quarter, 256), f32),
+            pltpu.VMEM((4, parts, 2 * quarter, 256), bf),
+            pltpu.VMEM((4, parts, 2 * quarter, 256), bf),
+            pltpu.VMEM((4, parts, quarter, 256), bf),
+            pltpu.VMEM((4, parts, quarter, 256), bf),
+            pltpu.VMEM((2, parts, quarter, 256), bf),
+            pltpu.VMEM((2, parts, quarter, 256), bf),
+            pltpu.VMEM((parts, 2 * quarter, 256), f32),
+            pltpu.VMEM((4, parts, 4 * per, 256), bf),
+            pltpu.VMEM((4, parts, 4 * per, 256), bf),
+            pltpu.VMEM((parts, 2, per, 256), bf),
+            pltpu.VMEM((parts, 2, per, 256), bf),
             pltpu.SemaphoreType.DMA,
-            pltpu.SemaphoreType.DMA((96,)),
+            pltpu.SemaphoreType.DMA((112,)),
             pltpu.SemaphoreType.DMA((64,)),
-            pltpu.SemaphoreType.DMA((4,)),
-            pltpu.SemaphoreType.DMA((4,)),
-            pltpu.SemaphoreType.DMA((2,)),
-            pltpu.SemaphoreType.DMA((4,)),
-            pltpu.SemaphoreType.DMA,
+            pltpu.SemaphoreType.DMA((3 + parts,)),
+            pltpu.SemaphoreType.DMA((4 * parts,)),
+            pltpu.SemaphoreType.DMA((2 * parts,)),
+            pltpu.SemaphoreType.DMA((4 * parts,)),
+            pltpu.SemaphoreType.DMA((parts,)),
         ],
         compiler_params=pltpu.CompilerParams(
             collective_id=0, has_side_effects=True, vmem_limit_bytes=48 * 1024 * 1024

time: 72 us -> 60.3 us (0.84)
  Pallas kernels: 68.6 us -> 56.9 us
    pallas_call x1, Pallas kernels: 68.6 us -> 56.9 us  [fused(): pl.pallas_call(functools.partial(kernel, per, width, ff, n_ep), out_shape...]
where the time goes in v3:
time: 60.3 us; the launch traced here: 60 us
  Pallas kernels  56.9 us (94%)
  local copies, waits for them, and re-layouts  3.11 us (5%)
    pallas_call x1, Pallas kernels, fused(): pl.pallas_call(functools.partial(kernel, per, width, ff, n_ep), out_shape...  56.9 us
    unnamed x5, local copies, waits for them, and re-layouts  3.11 us

profile of v3, /device:TPU:0, one launch (start us, length us, event | category | flops | bytes accessed | tf_op | source)
XLA Modules:
  0.0 60.0 jit_solution(13526524781424541568)
XLA Ops:
  0.0 0.8 %copy.5.routes = s32[2,16,8]{2,1,0:T(8,128)S(1)} copy(s32[2,16,8]{1,2,0:T(8,128)} %param.5) | data formatting | bytes 2048 | tf_op args[1]
  0.8 0.8 %copy.6.gates = f32[2,16,8]{2,1,0:T(8,128)S(1)} copy(f32[2,16,8]{1,2,0:T(8,128)} %param.6) | data formatting | bytes 2048 | tf_op args[2]
  1.5 0.0 copy-start
  1.5 0.9 %copy-done = bf16[2,16,3584]{2,1,0:T(8,128)(2,1)S(1)} copy-done((bf16[2,16,3584]{2,1,0:T(8,128)(2,1)S(1)}, bf16[2,16,3584]{2,1,0:T(8,128)(2,1)}, u32[]{:S(2)}) %copy-start) | copy-done | bytes 229400
  2.5 56.9 %shard_map.46 = bf16[2,16,1024]{2,1,0:T(8,128)(2,1)S(1)} custom-call(bf16[2,16,3584]{2,1,0:T(8,128)(2,1)S(1)} %copy-done, s32[2,16,8]{2,1,0:T(8,128)S(1)} %copy.5.routes, f32[2,16,8]{2,1,0:T(8,128)S(1)} %copy.6.gates, bf16[1,3584,1024]{2,1,0:T(8,128)(2,1)} %w_hbm.1), custom_call_target="tpu_custom_call" | custom-call | flops 7516192768 | bytes 7340032 | tf_op jit(solution)/shard_map/pallas_call | solution.py:266
  59.4 0.6 %copy.8 = bf16[2,16,1024]{2,1,0:T(8,128)(2,1)} copy(bf16[2,16,1024]{2,1,0:T(8,128)(2,1)S(1)} %shard_map.46) | data formatting | bytes 131072
Async XLA Ops:
  1.5 0.9 %copy-start = (bf16[2,16,3584]{2,1,0:T(8,128)(2,1)S(1)}, bf16[2,16,3584]{2,1,0:T(8,128)(2,1)}, u32[]{:S(2)}) copy-start(bf16[2,16,3584]{2,1,0:T(8,128)(2,1)} %tok.1) | copy-start | bytes 688132

commit v4 on v3

--- a/solution.py
+++ b/solution.py
@@ -41,7 +41,8 @@
         pl.semaphore_signal(barrier, inc=1, device_id={"ep": dev}, device_id_type=MESH)
 
     lane = lax.broadcasted_iota(jnp.int32, (per, 128), 1)
-    for h in range(2):
+
+    def stage(h):
         rows = pl.ds(pl.multiple_of(place(y, x, h, c, z) * per, per), per)
         for g in range(width // 128):
             v = tok[h, :, g * 128 : (g + 1) * 128].astype(jnp.float32)
@@ -59,6 +60,7 @@
         low = low - low.astype(jnp.bfloat16).astype(jnp.float32)
         got[rows, width : width + 128] = jnp.where(lane < experts, high, low).astype(jnp.bfloat16)
 
+    stage(0)
     pl.semaphore_wait(barrier, 6)
 
     copies, inner_copies = [], []
@@ -114,7 +116,7 @@
         def tile(col):
             cols = pl.ds(pl.multiple_of(col, 256), 256)
             v = jnp.dot(got[rows, :width], w[:, cols], preferred_element_type=jnp.float32)
-            return gate * (v / (1.0 + jnp.exp(-v)))
+            return (gate * (0.5 * v)) * (1.0 + jnp.tanh(0.5 * v))
 
         for j in range(parts):
             cs[u, j] = tile(oc * half + j * 256).astype(jnp.bfloat16)
@@ -129,13 +131,12 @@
                 mine[u, j] = tile(c * half + j * 256)
 
     def neighbours(k):
-        if k != 1:
-            spot = place(y, ox, 0, c, line[k])
-            arrive(spot)
-            pass_on(spot, [y_dev, c_dev])
-            spot = place(oy, x, 1, c, line[k])
-            arrive(spot)
-            pass_on(spot, [x_dev, c_dev])
+        spot = place(y, ox, 0, c, line[k])
+        arrive(spot)
+        pass_on(spot, [c_dev] if k == 1 else [y_dev, c_dev])
+        spot = place(oy, x, 1, c, line[k])
+        arrive(spot)
+        pass_on(spot, [c_dev] if k == 1 else [x_dev, c_dev])
         spot = place(y, ox, 1, c, line[k])
         arrive(spot)
         pass_on(spot, [c_dev])
@@ -151,6 +152,8 @@
 
     near, across = device(line[1], y, x, c), device(3 - z, y, x, c)
     for h in range(2):
+        if h == 1:
+            stage(1)
         spot = place(y, x, h, c, z)
         pass_on(spot, [near])
         inner_on(spot, across)
@@ -160,18 +163,13 @@
             spot = place(y, x, h, c, line[k])
             arrive(spot)
             inner_on(spot, across if k == 1 else near)
-            pass_on(spot, [x_dev, y_dev, c_dev] if k > 1 else [(y_dev, x_dev)[h], c_dev])
+            pass_on(spot, [x_dev, y_dev, c_dev])
         neighbours(k - 1)
-    pass_on(place(y, ox, 0, c, z), [near])
-    pass_on(place(oy, x, 1, c, z), [near])
     diagonal(0)
     w_copy.wait()
     sibling_line(y, x)
     compute(0, y, x)
     neighbours(3)
-    for spot in (place(y, ox, 0, c, line[1]), place(oy, x, 1, c, line[1])):
-        arrive(spot)
-        pass_on(spot, [c_dev])
     sibling_line(y, ox)
     compute(1, y, ox)
     diagonal(2)

time: 60.3 us -> 59.8 us (level)
  no operation moved by 1% of the time
where the time goes in v4:
time: 59.8 us; the launch traced here: 59.5 us
  Pallas kernels  56.4 us (94%)
  local copies, waits for them, and re-layouts  3.11 us (5%)
    pallas_call x1, Pallas kernels, fused(): pl.pallas_call(functools.partial(kernel, per, width, ff, n_ep), out_shape...  56.4 us
    unnamed x5, local copies, waits for them, and re-layouts  3.11 us

profile of v4, /device:TPU:0, one launch (start us, length us, event | category | flops | bytes accessed | tf_op | source)
XLA Modules:
  0.0 59.5 jit_solution(16289437792127450643)
XLA Ops:
  0.0 0.8 %copy.5.routes = s32[2,16,8]{2,1,0:T(8,128)S(1)} copy(s32[2,16,8]{1,2,0:T(8,128)} %param.5) | data formatting | bytes 2048 | tf_op args[1]
  0.8 0.8 %copy.6.gates = f32[2,16,8]{2,1,0:T(8,128)S(1)} copy(f32[2,16,8]{1,2,0:T(8,128)} %param.6) | data formatting | bytes 2048 | tf_op args[2]
  1.5 0.0 copy-start
  1.5 0.9 %copy-done = bf16[2,16,3584]{2,1,0:T(8,128)(2,1)S(1)} copy-done((bf16[2,16,3584]{2,1,0:T(8,128)(2,1)S(1)}, bf16[2,16,3584]{2,1,0:T(8,128)(2,1)}, u32[]{:S(2)}) %copy-start) | copy-done | bytes 229400
  2.5 56.4 %shard_map.46 = bf16[2,16,1024]{2,1,0:T(8,128)(2,1)S(1)} custom-call(bf16[2,16,3584]{2,1,0:T(8,128)(2,1)S(1)} %copy-done, s32[2,16,8]{2,1,0:T(8,128)S(1)} %copy.5.routes, f32[2,16,8]{2,1,0:T(8,128)S(1)} %copy.6.gates, bf16[1,3584,1024]{2,1,0:T(8,128)(2,1)} %w_hbm.1), custom_call_target="tpu_custom_call" | custom-call | flops 7516192768 | bytes 7340032 | tf_op jit(solution)/shard_map/pallas_call | solution.py:264
  58.9 0.6 %copy.8 = bf16[2,16,1024]{2,1,0:T(8,128)(2,1)} copy(bf16[2,16,1024]{2,1,0:T(8,128)(2,1)S(1)} %shard_map.46) | data formatting | bytes 131072
Async XLA Ops:
  1.5 0.9 %copy-start = (bf16[2,16,3584]{2,1,0:T(8,128)(2,1)S(1)}, bf16[2,16,3584]{2,1,0:T(8,128)(2,1)}, u32[]{:S(2)}) copy-start(bf16[2,16,3584]{2,1,0:T(8,128)(2,1)} %tok.1) | copy-start | bytes 688132

commit v5 on v4

--- a/solution.py
+++ b/solution.py
@@ -218,7 +218,7 @@
         for i, rows in ((0, lo), (1, hi)):
             landed(p2r.at[i, j], p2_sem.at[i * parts + j])
             tot[j, rows] = tot[j, rows] + p2r[i, j].astype(jnp.float32)
-        for k in range(1, 4):
+        for k in (2, 1, 3):
             for h in range(2):
                 for cc in range(2):
                     at = (h * 2 + cc) * per

time: 59.8 us -> 60.2 us (level)
  no operation moved by 1% of the time
where the time goes in v5:
time: 60.2 us; the launch traced here: 59.9 us
  Pallas kernels  56.8 us (94%)
  local copies, waits for them, and re-layouts  3.11 us (5%)
    pallas_call x1, Pallas kernels, fused(): pl.pallas_call(functools.partial(kernel, per, width, ff, n_ep), out_shape...  56.8 us
    unnamed x5, local copies, waits for them, and re-layouts  3.11 us

profile of v5, /device:TPU:0, one launch (start us, length us, event | category | flops | bytes accessed | tf_op | source)
XLA Modules:
  0.0 59.9 jit_solution(15016028724331110882)
XLA Ops:
  0.0 0.8 %copy.5.routes = s32[2,16,8]{2,1,0:T(8,128)S(1)} copy(s32[2,16,8]{1,2,0:T(8,128)} %param.5) | data formatting | bytes 2048 | tf_op args[1]
  0.8 0.8 %copy.6.gates = f32[2,16,8]{2,1,0:T(8,128)S(1)} copy(f32[2,16,8]{1,2,0:T(8,128)} %param.6) | data formatting | bytes 2048 | tf_op args[2]
  1.5 0.0 copy-start
  1.5 0.9 %copy-done = bf16[2,16,3584]{2,1,0:T(8,128)(2,1)S(1)} copy-done((bf16[2,16,3584]{2,1,0:T(8,128)(2,1)S(1)}, bf16[2,16,3584]{2,1,0:T(8,128)(2,1)}, u32[]{:S(2)}) %copy-start) | copy-done | bytes 229400
  2.5 56.8 %shard_map.46 = bf16[2,16,1024]{2,1,0:T(8,128)(2,1)S(1)} custom-call(bf16[2,16,3584]{2,1,0:T(8,128)(2,1)S(1)} %copy-done, s32[2,16,8]{2,1,0:T(8,128)S(1)} %copy.5.routes, f32[2,16,8]{2,1,0:T(8,128)S(1)} %copy.6.gates, bf16[1,3584,1024]{2,1,0:T(8,128)(2,1)} %w_hbm.1), custom_call_target="tpu_custom_call" | custom-call | flops 7516192768 | bytes 7340032 | tf_op jit(solution)/shard_map/pallas_call | solution.py:264
  59.3 0.6 %copy.8 = bf16[2,16,1024]{2,1,0:T(8,128)(2,1)} copy(bf16[2,16,1024]{2,1,0:T(8,128)(2,1)S(1)} %shard_map.46) | data formatting | bytes 131072
Async XLA Ops:
  1.5 0.9 %copy-start = (bf16[2,16,3584]{2,1,0:T(8,128)(2,1)S(1)}, bf16[2,16,3584]{2,1,0:T(8,128)(2,1)}, u32[]{:S(2)}) copy-start(bf16[2,16,3584]{2,1,0:T(8,128)(2,1)} %tok.1) | copy-start | bytes 688132
